TPU v7x, 32 devices: a whole 2x2x4 slice. The times are simulated.
32 devices in a mesh: seq: 8 (over z, x), batch: 4 (over y, core).
Axes of the slice: x: 2, y: 2, z: 4, core: 2. Of those that a mesh axis runs over, the one named last changes fastest.
Arguments:
- events: bfloat16 [4, 32768, 1, 256], P('batch', 'seq'), may hold values from -6 to 6
- spectral_filter: float32 [2, 32768, 256], P(None, None, 'seq'), may hold values from -6 to 6
- ln_gain: float32 [256], replicated, may hold values from 0.1 to 1.9
- w_in: bfloat16 [64, 1024, 256], P('seq', 'batch'), may hold values from -0.375 to 0.375
- w_out: bfloat16 [64, 1024, 256], P('seq', 'batch'), may hold values from -0.1875 to 0.1875
- gate_weight: bfloat16 [3, 256, 64], replicated, may hold values from -0.375 to 0.375
- gate_table: float32 [3, 16], replicated, may hold values from -4 to 4
- routes: int32 [4, 32768, 1, 1], P('batch', 'seq'), may hold values from 0 to 63; in each aligned block of 4096 rows (0 to 4095, 4096 to 8191, ..., all dimensions but the last counted through in order) at most 128 rows name the same one
- gate_index: int32 [4, 32768, 1, 3], P('batch', 'seq'), may hold values from 0 to 15
Outputs:
- task_out: bfloat16 [3, 4, 32768, 1, 256], P(None, 'batch', 'seq')
Inputs may be any that keep to these rules, and one draw needn't show every extreme that they name: `routes`: in each aligned block of 4096 rows (the events of one device) no expert is named by more than 128 rows; in some block one expert is named by exactly 128.
All inputs are finite; a program needn't handle non-finite values.
Results may differ from a plain program's by a relative error of at most 0.0072.
Values may be sent and summed in bfloat16 or wider, within the bound.
A program may use at most 128 MiB of HBM per device.

v0:
```python
import math

import jax
import jax.numpy as jnp
from jax import lax
from jax.sharding import PartitionSpec as P

EXPERTS = 64
TASKS = 3


HIGHEST = lax.Precision.HIGHEST


def split_length(length):
    factor = math.isqrt(length)
    while length % factor:
        factor -= 1
    return factor


def dft_table(points):
    indices = jnp.arange(points, dtype=jnp.int32)
    product = indices[:, None] * indices[None, :] % points
    angles = product.astype(jnp.float32) * (2.0 * math.pi / points)
    return (jnp.cos(angles), jnp.sin(angles))


def twiddle_table(outer_len, inner_len):
    length = outer_len * inner_len
    outer_idx = jnp.arange(outer_len, dtype=jnp.int32)
    inner_idx = jnp.arange(inner_len, dtype=jnp.int32)
    product = outer_idx[:, None] * inner_idx[None, :] % length
    angles = product.astype(jnp.float32) * (2.0 * math.pi / length)
    return (jnp.cos(angles)[:, :, None], jnp.sin(angles)[:, :, None])


def contract(values, matrix):
    return jnp.einsum("amb,mc->acb", values, matrix, precision=HIGHEST)


def spectral_pass(signal, filter_re, filter_im):
    length, col_count = signal.shape
    outer_len = split_length(length)
    inner_len = length // outer_len
    cos_outer, sin_outer = dft_table(outer_len)
    cos_inner, sin_inner = dft_table(inner_len)
    tw_cos, tw_sin = twiddle_table(outer_len, inner_len)
    flat_in = signal.reshape(outer_len, inner_len * col_count)
    part_re = jnp.dot(cos_outer, flat_in, precision=HIGHEST).reshape(
        outer_len, inner_len, col_count
    )
    part_im = -jnp.dot(sin_outer, flat_in, precision=HIGHEST).reshape(
        outer_len, inner_len, col_count
    )
    turn_re = part_re * tw_cos + part_im * tw_sin
    turn_im = part_im * tw_cos - part_re * tw_sin
    spec_re = contract(turn_re, cos_inner) + contract(turn_im, sin_inner)
    spec_im = contract(turn_im, cos_inner) - contract(turn_re, sin_inner)
    prod_re = spec_re * filter_re - spec_im * filter_im
    prod_im = spec_re * filter_im + spec_im * filter_re
    back_re = contract(prod_re, cos_inner) - contract(prod_im, sin_inner)
    back_im = contract(prod_im, cos_inner) + contract(prod_re, sin_inner)
    rot_re = (back_re * tw_cos - back_im * tw_sin).reshape(outer_len, inner_len * col_count)
    rot_im = (back_im * tw_cos + back_re * tw_sin).reshape(outer_len, inner_len * col_count)
    result = jnp.dot(cos_outer, rot_re, precision=HIGHEST) - jnp.dot(
        sin_outer, rot_im, precision=HIGHEST
    )
    return result.reshape(length, col_count) / length


def filter_layout(values, outer_len, inner_len, user_count):
    chan_dev = values.shape[1]
    turned = values.reshape(inner_len, outer_len, chan_dev).transpose(1, 0, 2)
    wide = turned[:, :, None, :]
    return wide.reshape(outer_len, inner_len, user_count * chan_dev)


def layer_norm(summed, gain_vec):
    centre = jnp.mean(summed, -1, keepdims=True, dtype=jnp.float32)
    square_mean = jnp.mean(jnp.square(summed.astype(jnp.float32)), -1, keepdims=True)
    spread_sq = jnp.maximum(square_mean - centre * centre, 0.0)
    return ((summed.astype(jnp.float32) - centre) * lax.rsqrt(spread_sq + 1e-05) * gain_vec).astype(
        jnp.bfloat16
    )


def build_slots(rows, targets, slot_total):
    row_count = rows.shape[0]
    owner_map = (
        jnp.full((slot_total,), row_count, jnp.int32)
        .at[targets]
        .set(jnp.arange(row_count, dtype=jnp.int32))
    )
    padded = jnp.concatenate([rows, jnp.zeros((1, rows.shape[1]), rows.dtype)], 0)
    return padded[owner_map]


def expert_ffn(normed, w_in, w_out):
    part_in = lax.all_gather(w_in, "batch", axis=1, tiled=True)
    part_out = lax.all_gather(w_out, "batch", axis=1, tiled=True)
    hidden = jnp.maximum(
        jnp.einsum("jsc,jhc->jsh", normed, part_in, preferred_element_type=jnp.float32), 0.0
    ).astype(jnp.bfloat16)
    summed = jnp.einsum("jsh,jhc->jsc", hidden, part_out, preferred_element_type=jnp.float32)
    return summed.astype(jnp.bfloat16)


def on_device(
    events, spectral_filter, ln_gain, w_in, w_out, gate_weight, gate_table, routes, gate_index
):
    n_seq = lax.axis_size("seq")
    len_dev = events.shape[1]
    user_count = events.shape[2]
    channels = events.shape[3]
    chan_dev = channels // n_seq
    length = len_dev * n_seq
    tok_count = len_dev * user_count
    capacity = max(2, 2 * tok_count // EXPERTS)
    col_count = user_count * chan_dev
    outer_len = split_length(length)
    inner_len = length // outer_len
    channel_view = lax.all_to_all(events, "seq", split_axis=3, concat_axis=1, tiled=True)
    filter_re = filter_layout(spectral_filter[0], outer_len, inner_len, user_count)
    filter_im = filter_layout(spectral_filter[1], outer_len, inner_len, user_count)
    signal = channel_view.reshape(length, col_count).astype(jnp.float32)
    filtered = spectral_pass(signal, filter_re, filter_im)
    summed_ch = (signal + filtered).astype(jnp.bfloat16).reshape(1, length, user_count, chan_dev)
    expert_ids = routes.reshape(tok_count)
    onehot = (expert_ids[:, None] == jnp.arange(EXPERTS, dtype=jnp.int32)[None, :]).astype(
        jnp.int32
    )
    earlier = jnp.cumsum(onehot, 0) - onehot
    rank_vals = jnp.sum(earlier * onehot, 1)
    slot_index = expert_ids * capacity + rank_vals
    returned = lax.all_to_all(summed_ch, "seq", split_axis=1, concat_axis=3, tiled=True)
    normed = layer_norm(returned, ln_gain).reshape(tok_count, channels)
    outgoing = build_slots(normed, slot_index, EXPERTS * capacity).reshape(
        EXPERTS, capacity, channels
    )
    arrived = lax.all_to_all(outgoing, "seq", split_axis=0, concat_axis=1, tiled=True)
    expert_out = expert_ffn(arrived, w_in, w_out)
    result_slots = lax.all_to_all(expert_out, "seq", split_axis=1, concat_axis=0, tiled=True)
    gate_cols = gate_weight.transpose(1, 0, 2).reshape(channels, TASKS * EXPERTS)
    all_scores = jnp.dot(normed, gate_cols, preferred_element_type=jnp.float32).reshape(
        tok_count, TASKS, EXPERTS
    )
    pick = jnp.broadcast_to(expert_ids[:, None, None], (tok_count, TASKS, 1))
    chosen = jnp.take_along_axis(all_scores, pick, axis=2)[:, :, 0].astype(jnp.bfloat16)
    expert_rows = result_slots.reshape(-1, channels)[slot_index].astype(jnp.float32)
    lookup = gate_index.reshape(tok_count, TASKS)
    matches = lookup[:, :, None] == jnp.arange(gate_table.shape[1], dtype=jnp.int32)[None, None, :]
    table_bias = jnp.sum(jnp.where(matches, gate_table[None], 0.0), -1)
    gate_vals = jax.nn.sigmoid(chosen.astype(jnp.float32) + table_bias)
    task_out = (gate_vals.T[:, :, None] * expert_rows[None]).astype(jnp.bfloat16)
    return task_out.reshape(TASKS, 1, len_dev, user_count, channels)


def solution(mesh):
    in_specs = (
        P("batch", "seq", None, None),
        P(None, None, "seq"),
        P(),
        P("seq", "batch", None),
        P("seq", "batch", None),
        P(),
        P(),
        P("batch", "seq", None, None),
        P("batch", "seq", None, None),
    )
    out_specs = P(None, "batch", "seq", None, None)
    return jax.shard_map(
        on_device, mesh=mesh, in_specs=in_specs, out_specs=out_specs, check_vma=False
    )
```

profile of v0, /device:TPU:0, one launch (start us, length us, event | category | flops | bytes accessed | tf_op | source)
XLA Modules:
  0.0 1147.9 jit_solution(368484177872079350)
XLA Ops:
  6.5 9.9 copy.130
  16.9 13.4 %reduce.11 = bf16[256,4096]{1,0:T(8,128)(2,1)S(1)} reduce(bf16[256,1,1,4096]{3,2,1,0:T(2,128)(2,1)} %bitcast.183, bf16[]{:T(256)} %broadcast.434), dimensions={1,2}, to_apply=%bitcast.152.reduce_sub_computation | reduce | bytes 4194306
  34.2 7.3 all-to-all-start
  51.4 38.2 %all-to-all-done = bf16[8,2,65536]{2,1,0:T(2,128)(2,1)S(1)} async-done(((bf16[8,2,65536]{2,1,0:T(2,128)(2,1)}), bf16[8,2,65536]{2,1,0:T(2,128)(2,1)S(1)}, u32[]{:S(2)}, u32[]{:S(2)}) %all-to-all-start) | async-done | bytes 2097184 | tf_op jit(solution)/shard_map/all_to_all | solution.py:123
  104.6 11.7 %reshape.446 = bf16[128,8192]{1,0:T(8,128)(2,1)} reshape(bf16[1,8,4096,1,32]{4,2,1,3,0:T(8,128)(2,1)} %copy.132) | data formatting | bytes 4194304 | tf_op jit(solution)/shard_map/reshape | solution.py:49
  130.5 7.7 fusion.39
  138.2 7.5 convolution_add_fusion
  145.7 11.4 fusion.5
  157.1 7.9 fusion.11
  165.0 8.1 fusion.9
  175.7 8.1 fusion.18
  183.7 12.2 %fusion.8 = (f32[128,256,32]{1,0,2:T(8,128)}, f32[128,256,32]{1,0,2:T(8,128)}) fusion(f32[256,128,32]{0,1,2:T(8,128)S(1)} %fusion.18, f32[128,256]{1,0:T(8,128)S(1)} %get-tuple-element.15, f32[128,256]{1,0:T(8,128)S(1)} %get-tuple-element.16, f32[256,128,32]{0,1,2:T(8,128)S(1)} %fusion.9, f32[256,128,32]{1,0,2:T(8,128)S(1)} %get-tuple-element.7), kind=kOutput, calls=%fused_computation.21 | convolution fusion | flops 3229483008 | bytes 21233664 | tf_op jit(solution)/shard_map/amb,mc->acb/dot_general | solution.py:39
  201.4 8.0 fusion.90
  215.0 9.5 fusion.4
  224.5 10.8 div.19
  235.3 11.6 %copy.146 = f32[1,32768,1,32]{1,3,2,0:T(8,128)} copy(f32[1,32768,1,32]{3,1,2,0:T(8,128)} %div.19) | data formatting | bytes 8388608 | tf_op jit(solution)/shard_map/div | solution.py:69
  250.7 25.2 %copy.147 = bf16[1,32768,1,32]{3,2,0,1:T(2,128)(2,1)} copy(bf16[1,32768,1,32]{1,3,2,0:T(8,128)(2,1)S(1)} %add_convert_fusion) | data formatting | bytes 4194304 | tf_op jit(solution)/shard_map/convert_element_type | solution.py:128
  275.9 179.1 %reduce.12 = bf16[32768,32]{1,0:T(8,128)(2,1)} reduce(bf16[32768,1,1,32]{3,2,1,0:T(2,128)(2,1)} %bitcast.174, bf16[]{:T(256)} %broadcast.434), dimensions={1,2}, to_apply=%bitcast.154.reduce_sub_computation | reduce | bytes 4194306
  455.0 11.2 reshape.502
  471.8 32.4 %reduce-window.6 = s32[64,32,128]{2,1,0:T(8,128)S(1)} reduce-window(s32[64,32,128]{2,1,0:T(8,128)} %fusion.37, s32[]{:T(128)} %constant.74.clone.1), window={size=1x1x128 pad=0_0x0_0x127_0}, to_apply=%region_5.6 | reduce-window | flops 33292288 | bytes 2097156 | tf_op jit(solution)/shard_map/reduce-window
  508.6 15.5 %scatter_custom_fusion = s32[8192]{0:T(1024)S(1)} fusion(s32[4096]{0:T(1024)S(1)} %bitcast.202, s32[4096]{0:T(1024)S(1)} %iota.49, s32[]{:T(128)} %constant.92.clone.1), kind=kCustom, calls=%fused_computation.132 | custom fusion | bytes 32772 | tf_op jit(solution)/shard_map/scatter | solution.py:93
  524.2 10.2 reshape.503
  534.3 244.9 %convert_reduce_fusion = (f32[32768]{0:T(1024)S(1)}, f32[32768]{0:T(1024)S(1)}) fusion(bf16[32768,1,1,32]{3,2,1,0:T(2,128)(2,1)} %reshape.503), kind=kLoop, calls=%fused_computation.139 | loop fusion | flops 4128768 | bytes 2359296 | tf_op jit(solution)/shard_map/reduce_sum | solution.py:80
  779.4 19.8 %bitcast_convert_fusion = f32[1,32768,1,32]{3,2,0,1:T(1,128)} fusion(bf16[32768,1,1,32]{3,2,1,0:T(2,128)(2,1)} %reshape.503), kind=kLoop, calls=%fused_computation.189 | loop fusion | flops 1048576 | bytes 6291456 | tf_op jit(solution)/shard_map/convert_element_type | solution.py:83
  799.2 11.7 %copy.169 = f32[1,8,4096,1,32]{2,1,4,3,0:T(8,128)} copy(f32[1,8,4096,1,32]{4,2,1,3,0:T(8,128)} %bitcast.173) | data formatting | bytes 8388608 | tf_op jit(solution)/shard_map/convert_element_type | solution.py:83
  810.9 6.5 copy.149
  826.3 33.2 %gather_fusion = bf16[8192,256]{1,0:T(8,128)(2,1)} fusion(bf16[4097,256]{1,0:T(8,128)(2,1)S(1)} %concatenate.3, s32[8192]{0:T(1024)S(1)} %fusion.87), kind=kCustom, calls=%fused_computation | custom fusion | bytes 8421376 | tf_op jit(solution)/shard_map/gather | solution.py:96
  866.2 92.1 %all-to-all-done.2 = bf16[64,128,256]{2,1,0:T(8,128)(2,1)} async-done(((bf16[64,128,256]{2,1,0:T(8,128)(2,1)}), bf16[64,128,256]{2,1,0:T(8,128)(2,1)}, u32[]{:S(2)}, u32[]{:S(2)}) %all-to-all-start.2) | async-done | bytes 4194336 | tf_op jit(solution)/shard_map/all_to_all | solution.py:141
  963.1 13.3 %fusion.17 = bf16[8,1024,256]{2,1,0:T(8,128)(2,1)} fusion(bf16[8,1024,256]{2,1,0:T(8,128)(2,1)} %all-gather.5.cloned.1.call-done, bf16[8,1024,256]{2,1,0:T(8,128)(2,1)} %bitcast.189, bf16[8,1024,256]{2,1,0:T(8,128)(2,1)} %all-gather.3.cloned.1.call-done), kind=kOutput, calls=%fused_computation.40 | convolution fusion | flops 8608808960 | bytes 16777216 | tf_op jit(solution)/shard_map/jsh,jhc->jsc/dot_general | solution.py:105
  976.3 6.6 copy.158
  994.8 117.2 %gather_fusion.2 = bf16[12288]{0:T(1024)(128)(2,1)S(1)} fusion(bf16[4096,3,64]{0,2,1:T(8,128)(2,1)S(1)} %fusion.25, s32[12288]{0:T(1024)S(1)} %reshape.476), kind=kCustom, calls=%fused_computation.2 | custom fusion | bytes 196608 | tf_op jit(solution)/shard_map/jit(take_along_axis)/gather | solution.py:149
  1120.7 15.7 %gather_fusion.1 = bf16[4096,256]{1,0:T(8,128)(2,1)S(1)} fusion(bf16[8192,256]{1,0:T(8,128)(2,1)} %bitcast.172, s32[4096]{0:T(1024)S(1)} %copy-done.9), kind=kCustom, calls=%fused_computation.1 | custom fusion | bytes 4210688 | tf_op jit(solution)/shard_map/gather | solution.py:150
  (95 shorter events, 115.8 us)
Async XLA Ops:
  6.5 985.3 %copy-start = (bf16[3,256,64]{1,2,0:T(8,128)(2,1)S(1)}, bf16[3,256,64]{1,2,0:T(8,128)(2,1)}, u32[]{:S(2)}) copy-start(bf16[3,256,64]{1,2,0:T(8,128)(2,1)} %param.14) | copy-start | bytes 294916
  34.2 55.5 %all-to-all-start = ((bf16[8,2,65536]{2,1,0:T(2,128)(2,1)}), bf16[8,2,65536]{2,1,0:T(2,128)(2,1)S(1)}, u32[]{:S(2)}, u32[]{:S(2)}) async-start(bf16[8,2,65536]{2,1,0:T(2,128)(2,1)} %reshape.500), calls=%async_computation | async-start | bytes 4194304 | tf_op jit(solution)/shard_map/all_to_all | solution.py:123
  98.5 6.1 copy-start.2
  165.0 8.1 copy-start.3
  246.9 3.4 copy-start.4
  466.1 4.5 copy-start.5
  466.1 58.0 %all-to-all-start.1 = ((bf16[8,2,65536]{2,1,0:T(2,128)(2,1)}), bf16[8,2,65536]{2,1,0:T(2,128)(2,1)S(1)}, u32[]{:S(2)}, u32[]{:S(2)}) async-start(bf16[8,2,65536]{2,1,0:T(2,128)(2,1)} %reshape.502), calls=%async_computation.1 | async-start | bytes 4194304 | tf_op jit(solution)/shard_map/all_to_all | solution.py:136
  469.9 493.1 %all-gather.3.cloned.1.call-start = ((), (), s32[]{:S(2)}) async-start(), calls=%async_computation.4 | async-start | bytes 5242880 | tf_op jit(solution)/shard_map/all_gather | solution.py:100
  817.5 5.6 copy-start.12
  859.5 98.9 %all-to-all-start.2 = ((bf16[64,128,256]{2,1,0:T(8,128)(2,1)}), bf16[64,128,256]{2,1,0:T(8,128)(2,1)}, u32[]{:S(2)}, u32[]{:S(2)}) async-start(bf16[64,128,256]{2,1,0:T(8,128)(2,1)} %bitcast.187), calls=%async_computation.2 | async-start | bytes 8388608 | tf_op jit(solution)/shard_map/all_to_all | solution.py:141
  865.5 97.6 %all-gather.5.cloned.1.call-start = ((), (), s32[]{:S(2)}) async-start(), calls=%async_computation.5 | async-start | bytes 5242880 | tf_op jit(solution)/shard_map/all_gather | solution.py:101
  982.9 132.4 %all-to-all-start.3 = ((bf16[8,1024,256]{2,0,1:T(8,128)(2,1)}), bf16[8,1024,256]{2,0,1:T(8,128)(2,1)}, u32[]{:S(2)}, u32[]{:S(2)}) async-start(bf16[8,1024,256]{2,0,1:T(8,128)(2,1)} %copy.158), calls=%async_computation.3 | async-start | bytes 8388608 | tf_op jit(solution)/shard_map/all_to_all | solution.py:143
  987.7 2.6 copy-start.10
  987.7 2.6 copy-start.13
  987.7 7.1 copy-start.11
  987.7 7.1 copy-start.8
  994.8 119.7 %copy-start.6 = (s32[1,4096,1,1]{1,3,2,0:T(1,128)S(1)}, s32[1,4096,1,1]{1,3,2,0:T(1,128)}, u32[]{:S(2)}) copy-start(s32[1,4096,1,1]{1,3,2,0:T(1,128)} %param.16) | copy-start | bytes 49156
  994.8 119.7 %copy-start.7 = (f32[4096,3]{0,1:T(4,128)S(1)}, f32[4096,3]{0,1:T(4,128)}, u32[]{:S(2)}) copy-start(f32[4096,3]{0,1:T(4,128)} %select_reduce_fusion) | copy-start | bytes 147460
  1115.4 5.3 copy-start.9
  1136.4 4.4 copy-start.1
Sparse Core Ops, SparseCore 0:
  472.3 35.9 all-gather.2
  867.9 35.9 all-gather.4
where the time goes:
time: 1160 us; the launch traced here: 1150 us
  other arithmetic  506 us (44%)
  local copies, waits for them, and re-layouts  367 us (32%)
  waiting for transfers between devices  132 us (11%)
  matrix products  107 us (9%)
  starting transfers between devices  21.8 us (2%)
  between operations  14.1 us (1%)
    reduce_sum x2, other arithmetic, layer_norm(): centre = jnp.mean(summed, -1, keepdims=True, dtype=jnp.float32)  245 us
    unnamed x3, other arithmetic  195 us
    gather x5, local copies, waits for them, and re-layouts, on_device(): jnp.take_along_axis(all_scores, pick, axis=2)[:, :, 0].astype(jnp.bfloat16)  122 us
    all_to_all x1, waiting for transfers between devices, on_device(): lax.all_to_all(outgoing, 'seq', split_axis=0, concat_axis=1, tiled=True)  92.1 us
    dot_general x8, matrix products, contract(): return jnp.einsum('amb,mc->acb', values, matrix, precision=HIGHEST)  68.3 us
    unnamed x42, local copies, waits for them, and re-layouts  54.9 us
    all_to_all x1, waiting for transfers between devices, on_device(): lax.all_to_all(events, 'seq', split_axis=3, concat_axis=1, tiled=True)  38.2 us
    gather x1, local copies, waits for them, and re-layouts, build_slots(): return padded[owner_map]  33.2 us
  transfers between devices with their start and end apart: 6, of which 2 were waited for; matrix products, arithmetic and copies ran while one was open for 46% of the time, Pallas kernels for 0%

commit v1 on v0

v1 whole, which is shorter than its diff:
```python
import functools
import math

import jax
import jax.numpy as jnp
import numpy as np
from jax import lax
from jax.experimental import pallas as pl
from jax.experimental.pallas import tpu as pltpu
from jax.sharding import PartitionSpec as P

EXPERTS = 64
TASKS = 3
INNER = 256
LANES = 128
VMEM_BYTES = 56 * 2**20
F32 = jnp.float32
BF16 = jnp.bfloat16


def params():
    return pltpu.CompilerParams(vmem_limit_bytes=VMEM_BYTES)


def dot_nt(a, b):
    return lax.dot_general(a, b, (((1,), (1,)), ((), ())), preferred_element_type=F32)


def dot_nn(a, b):
    return jnp.dot(a, b, preferred_element_type=F32)


def tables(length):
    outer = length // INNER

    def angles(rows, cols, points):
        product = np.outer(np.arange(rows), np.arange(cols)) % points
        return product * (2.0 * np.pi / points)

    first = angles(outer, outer, outer)
    inner = angles(INNER, INNER, INNER)
    turn = angles(outer, INNER, length)
    c1, s1, c2, s2 = np.cos(first), np.sin(first), np.cos(inner), np.sin(inner)
    f1 = np.concatenate([c1, -s1], 0)
    m2 = np.block([[c2, s2], [-s2, c2]])
    m3 = np.block([[c2, -s2], [s2, c2]])
    f4 = np.concatenate([c1, -s1], 1) / length
    bf = lambda a: jnp.asarray(a.astype(np.float32)).astype(BF16)
    fl = lambda a: jnp.asarray(a.astype(np.float32))
    return (
        bf(f1), bf(m2), bf(m3), bf(f4),
        fl(np.cos(turn)), fl(np.sin(turn)), fl(np.cos(turn).T), fl(np.sin(turn).T),
    )


def turn_kernel(blocks, x_ref, out_ref, low, high):
    def step(j, _):
        rows = x_ref[pl.ds(pl.multiple_of(j * INNER, INNER), INNER), :]
        turned = rows.astype(F32).T
        low[pl.ds(j, LANES, stride=blocks), :] = turned[:, :LANES]
        high[pl.ds(j, LANES, stride=blocks), :] = turned[:, LANES:]
        return 0

    lax.fori_loop(0, blocks, step, 0, unroll=2)
    out_ref[:, :LANES] = low[...].astype(BF16)
    out_ref[:, LANES:] = high[...].astype(BF16)


def turn(events):
    tokens, channels = events.shape
    blocks = tokens // INNER
    rows = LANES * blocks
    return pl.pallas_call(
        functools.partial(turn_kernel, blocks),
        grid=(channels // LANES,),
        in_specs=[pl.BlockSpec((tokens, LANES), lambda i: (0, i))],
        out_specs=pl.BlockSpec((rows, INNER), lambda i: (i, 0)),
        out_shape=jax.ShapeDtypeStruct((channels * blocks, INNER), BF16),
        scratch_shapes=[pltpu.VMEM((rows, LANES), F32), pltpu.VMEM((rows, LANES), F32)],
        compiler_params=params(),
        name="turn",
    )(events)


def spectral_kernel(
    chans, outer, x_ref, h_ref, f1_ref, m2_ref, m3_ref, f4_ref, tc, ts, tct, tst, out_ref,
    y_ref, g_ref,
):
    x_all = x_ref[...]
    for c in range(chans):
        x = x_all[:, c].reshape(outer, INNER)
        a = dot_nn(f1_ref[...], x)
        re, im = a[:outer], a[outer:]
        rows = slice(c * outer, (c + 1) * outer)
        y_ref[rows, :INNER] = (re * tc[...] + im * ts[...]).astype(BF16)
        y_ref[rows, INNER:] = (im * tc[...] - re * ts[...]).astype(BF16)
    z = dot_nt(m2_ref[...], y_ref[...])
    for c in range(chans):
        cols = slice(c * outer, (c + 1) * outer)
        zr, zi = z[:INNER, cols], z[INNER:, cols]
        hr, hi = h_ref[0, c], h_ref[1, c]
        g_ref[:INNER, cols] = (zr * hr - zi * hi).astype(BF16)
        g_ref[INNER:, cols] = (zr * hi + zi * hr).astype(BF16)
    u = dot_nn(m3_ref[...], g_ref[...])
    for c in range(chans):
        cols = slice(c * outer, (c + 1) * outer)
        ur, ui = u[:INNER, cols], u[INNER:, cols]
        v = jnp.concatenate(
            [
                (ur * tct[...] - ui * tst[...]).astype(BF16),
                (ui * tct[...] + ur * tst[...]).astype(BF16),
            ],
            1,
        )
        y = dot_nt(f4_ref[...], v)
        x = x_all[:, c].reshape(outer, INNER)
        total = (x.astype(F32) + y).astype(BF16)
        out_ref[:, c] = total.reshape(out_ref.shape[0], out_ref.shape[2], INNER)


def spectral(x, spectral_filter):
    parts, chan_dev, blocks, _ = x.shape
    length = parts * blocks * INNER
    outer = length // INNER
    chans = math.gcd(chan_dev, 4)
    consts = tables(length)
    filt = spectral_filter.transpose(0, 2, 1).reshape(2, chan_dev, INNER, outer)
    whole = lambda a: pl.BlockSpec(a.shape, lambda i: (0,) * a.ndim)
    x_spec = pl.BlockSpec((parts, chans, blocks, INNER), lambda i: (0, i, 0, 0))
    return pl.pallas_call(
        functools.partial(spectral_kernel, chans, outer),
        grid=(chan_dev // chans,),
        in_specs=[x_spec, pl.BlockSpec((2, chans, INNER, outer), lambda i: (0, i, 0, 0))]
        + [whole(a) for a in consts],
        out_specs=x_spec,
        out_shape=jax.ShapeDtypeStruct(x.shape, BF16),
        scratch_shapes=[
            pltpu.VMEM((chans * outer, 2 * INNER), BF16),
            pltpu.VMEM((2 * INNER, chans * outer), BF16),
        ],
        compiler_params=params(),
        name="spectral",
    )(x, filt, *consts)


def slot_kernel(capacity, routes_ref, slot_ref):
    tokens = routes_ref.shape[1]
    row = lax.broadcasted_iota(jnp.int32, (INNER, INNER), 0)
    col = lax.broadcasted_iota(jnp.int32, (INNER, INNER), 1)
    before = (row < col).astype(F32).astype(BF16)
    expert = lax.broadcasted_iota(jnp.int32, (EXPERTS, INNER), 0)
    base = (lax.broadcasted_iota(jnp.int32, (EXPERTS, 1), 0) * capacity).astype(F32)
    for j in range(tokens // INNER):
        cols = slice(j * INNER, (j + 1) * INNER)
        hot = (expert == routes_ref[:, cols]).astype(F32)
        rank = dot_nn(hot.astype(BF16), before)
        slot_ref[:, cols] = jnp.sum(hot * (rank + base), 0, keepdims=True).astype(jnp.int32)
        base = base + jnp.sum(hot, 1, keepdims=True)


def slots_of(routes, capacity):
    return pl.pallas_call(
        functools.partial(slot_kernel, capacity),
        out_shape=jax.ShapeDtypeStruct(routes.shape, jnp.int32),
        compiler_params=params(),
        name="slots",
    )(routes)


def norm_kernel(
    blocks, x_ref, gain_ref, gw_ref, routes_ref, gi_ref, slot_ref, table_ref,
    out_ref, gate_ref, low, high, rows_ref, spread,
):
    channels = gain_ref.shape[1]
    low[...] = x_ref[:, :LANES].astype(F32)
    high[...] = x_ref[:, LANES:].astype(F32)
    expert = lax.broadcasted_iota(jnp.int32, (EXPERTS, INNER), 0)

    def step(j, _):
        start = pl.multiple_of(j * INNER, INNER)
        t = jnp.concatenate(
            [
                low[pl.ds(j, channels, stride=blocks), :],
                high[pl.ds(j, channels, stride=blocks), :],
            ],
            1,
        )
        centre = jnp.sum(t, 0, keepdims=True) * (1.0 / channels)
        away = t - centre
        var = jnp.sum(away * away, 0, keepdims=True) * (1.0 / channels)
        scaled = away * lax.rsqrt(var + 1e-05)
        normed = (scaled.T * gain_ref[...]).astype(BF16)
        rows_ref[...] = normed.astype(F32)
        scores = dot_nt(gw_ref[...], normed)
        hot = expert == routes_ref[:, pl.ds(start, INNER)]
        for task in range(TASKS):
            part = scores[task * EXPERTS:(task + 1) * EXPERTS]
            chosen = jnp.sum(jnp.where(hot, part, 0.0), 0, keepdims=True)
            index = gi_ref[task:task + 1, pl.ds(start, INNER)]
            bias = jnp.zeros((1, INNER), F32)
            for entry in range(table_ref.shape[1]):
                bias = jnp.where(index == entry, table_ref[task, entry], bias)
            logit = chosen.astype(BF16).astype(F32) + bias
            gate_ref[task:task + 1, pl.ds(start, INNER)] = jax.nn.sigmoid(logit)

        def move(i, _):
            for u in range(16):
                n = i * 16 + u
                spread[pl.ds(slot_ref[0, start + n], 1), :] = rows_ref[pl.ds(n, 1), :]
            return 0

        lax.fori_loop(0, INNER // 16, move, 0)
        return 0

    lax.fori_loop(0, blocks, step, 0)
    out_ref[...] = spread[...].astype(BF16)


def norm_and_send(x, gain, gate_cols, routes, index, slot, table, slot_total):
    channels = gain.shape[1]
    blocks = x.shape[0] // channels
    tokens = blocks * INNER
    vmem = pl.BlockSpec(memory_space=pltpu.VMEM)
    smem = pl.BlockSpec(memory_space=pltpu.SMEM)
    return pl.pallas_call(
        functools.partial(norm_kernel, blocks),
        in_specs=[vmem] * 5 + [smem] * 2,
        out_specs=[vmem, vmem],
        out_shape=[
            jax.ShapeDtypeStruct((slot_total, channels), BF16),
            jax.ShapeDtypeStruct((8, tokens), F32),
        ],
        scratch_shapes=[
            pltpu.VMEM((x.shape[0], LANES), F32),
            pltpu.VMEM((x.shape[0], LANES), F32),
            pltpu.VMEM((INNER, channels), F32),
            pltpu.VMEM((slot_total, channels), F32),
        ],
        compiler_params=params(),
        name="norm",
    )(x, gain, gate_cols, routes, index, slot, table)


def expert_kernel(x_ref, w_in_ref, w_out_ref, out_ref):
    x = x_ref[...].reshape(-1, x_ref.shape[-1])
    w_in = w_in_ref[...].reshape(-1, w_in_ref.shape[-1])
    w_out = w_out_ref[...].reshape(-1, w_out_ref.shape[-1])
    hidden = jnp.maximum(dot_nt(x, w_in), 0.0).astype(BF16)
    out_ref[...] = dot_nn(hidden, w_out).astype(BF16).reshape(out_ref.shape)


def experts(x, w_in, w_out):
    sources, count, capacity, channels = x.shape
    shares, _, hid, _ = w_in.shape
    x_spec = pl.BlockSpec((sources, 1, capacity, channels), lambda e: (0, e, 0, 0))
    w_spec = pl.BlockSpec((shares, 1, hid, channels), lambda e: (0, e, 0, 0))
    return pl.pallas_call(
        expert_kernel,
        grid=(count,),
        in_specs=[x_spec, w_spec, w_spec],
        out_specs=x_spec,
        out_shape=jax.ShapeDtypeStruct(x.shape, BF16),
        compiler_params=params(),
        name="experts",
    )(x, w_in, w_out)


def finish_kernel(res_ref, gate_ref, slot_ref, out_ref, wide, rows_ref):
    j = pl.program_id(0)

    @pl.when(j == 0)
    def _():
        wide[...] = res_ref[...].astype(F32)

    start = j * INNER

    def move(i, _):
        for u in range(16):
            n = i * 16 + u
            rows_ref[pl.ds(n, 1), :] = wide[pl.ds(slot_ref[0, start + n], 1), :]
        return 0

    lax.fori_loop(0, INNER // 16, move, 0)
    gates = gate_ref[...].T
    rows = rows_ref[...]
    for task in range(TASKS):
        out_ref[task] = (gates[:, task:task + 1] * rows).astype(BF16)


def finish(results, gates, slot):
    slot_total, channels = results.shape
    tokens = gates.shape[1]
    return pl.pallas_call(
        finish_kernel,
        grid=(tokens // INNER,),
        in_specs=[
            pl.BlockSpec((slot_total, channels), lambda j: (0, 0)),
            pl.BlockSpec((8, INNER), lambda j: (0, j)),
            pl.BlockSpec(memory_space=pltpu.SMEM),
        ],
        out_specs=pl.BlockSpec((TASKS, INNER, channels), lambda j: (0, j, 0)),
        out_shape=jax.ShapeDtypeStruct((TASKS, tokens, channels), BF16),
        scratch_shapes=[
            pltpu.VMEM((slot_total, channels), F32),
            pltpu.VMEM((INNER, channels), F32),
        ],
        compiler_params=params(),
        name="finish",
    )(results, gates, slot)


def on_device(
    events, spectral_filter, ln_gain, w_in, w_out, gate_weight, gate_table, routes, gate_index
):
    n_seq = lax.axis_size("seq")
    _, len_dev, user_count, channels = events.shape
    chan_dev = channels // n_seq
    blocks = len_dev // INNER
    capacity = max(2, 2 * len_dev // EXPERTS)
    exp_dev = w_in.shape[0]
    route_row = routes.reshape(1, len_dev)
    index_rows = gate_index.reshape(len_dev, TASKS).T
    gate_cols = gate_weight.transpose(0, 2, 1).reshape(TASKS * EXPERTS, channels)
    all_in = lax.all_gather(w_in, "batch", axis=0, tiled=False)
    all_out = lax.all_gather(w_out, "batch", axis=0, tiled=False)

    turned = turn(events.reshape(len_dev, channels)).reshape(n_seq, chan_dev, blocks, INNER)
    history = lax.all_to_all(turned, "seq", split_axis=0, concat_axis=0, tiled=True)
    slot = slots_of(route_row, capacity)
    if blocks % 16:
        merged = history.transpose(1, 0, 2, 3).reshape(1, chan_dev, n_seq * blocks, INNER)
        summed = spectral(merged, spectral_filter)
        summed = summed.reshape(chan_dev, n_seq, blocks, INNER).transpose(1, 0, 2, 3)
    else:
        summed = spectral(history, spectral_filter)
    returned = lax.all_to_all(summed, "seq", split_axis=0, concat_axis=0, tiled=True)
    outgoing, gates = norm_and_send(
        returned.reshape(channels * blocks, INNER),
        ln_gain.reshape(1, channels),
        gate_cols,
        route_row,
        index_rows,
        slot,
        gate_table,
        EXPERTS * capacity,
    )
    arrived = lax.all_to_all(
        outgoing.reshape(n_seq, exp_dev, capacity, channels),
        "seq", split_axis=0, concat_axis=0, tiled=True,
    )
    done = experts(arrived, all_in, all_out)
    results = lax.all_to_all(done, "seq", split_axis=0, concat_axis=0, tiled=True)
    task_out = finish(results.reshape(EXPERTS * capacity, channels), gates, slot)
    return task_out.reshape(TASKS, 1, len_dev, user_count, channels)


def solution(mesh):
    in_specs = (
        P("batch", "seq", None, None),
        P(None, None, "seq"),
        P(),
        P("seq", "batch", None),
        P("seq", "batch", None),
        P(),
        P(),
        P("batch", "seq", None, None),
        P("batch", "seq", None, None),
    )
    out_specs = P(None, "batch", "seq", None, None)
    return jax.shard_map(
        on_device, mesh=mesh, in_specs=in_specs, out_specs=out_specs, check_vma=False
    )
```

time: 1160 us -> 402 us (0.35); the launches traced: 1150 us -> 402 us
  other arithmetic: 506 us -> 0 us
  local copies, waits for them, and re-layouts: 367 us -> 11.4 us
  matrix products: 107 us -> 0 us
  blocking collectives: 0 us -> 97.3 us
  Pallas kernels: 0 us -> 85.2 us
  waiting for transfers between devices: 132 us -> 178 us
    reduce_sum x5 -> x0, other arithmetic: 247 us -> none  [the longest x2 245 us: layer_norm(): centre = jnp.mean(summed, -1, keepdims=True, dtype=jnp.float32)]
    unnamed x3 -> x0, other arithmetic: 195 us -> none
    gather x7 -> x0, local copies, waits for them, and re-layouts: 171 us -> none  [the longest x5 122 us: on_device(): jnp.take_along_axis(all_scores, pick, axis=2)[:, :, 0].astype(jnp.bfloat16)]
    dot_general x14 -> x0, matrix products: 107 us -> none  [the longest x8 68.3 us: contract(): return jnp.einsum('amb,mc->acb', values, matrix, precision=HIGHEST)]
    all_to_all x0 -> x1, blocking collectives: none -> 97.3 us  [on_device(): lax.all_to_all(done, 'seq', split_axis=0, concat_axis=0, tiled=True)]
    pallas_call x0 -> x6, Pallas kernels: none -> 85.2 us  [the longest x1 26.3 us: norm_and_send(): pl.pallas_call(functools.partial(norm_kernel, blocks), in_specs=[vmem] *...]
    convert_element_type x6 -> x0, local copies, waits for them, and re-layouts: 58.2 us -> none  [the longest x1 25.2 us: on_device(): (signal + filtered).astype(jnp.bfloat16)]
    unnamed x42 -> x8, local copies, waits for them, and re-layouts: 54.9 us -> 11.4 us
  transfers between devices with their start and end apart: 6 -> 5, of which waited for: 2 -> 4; matrix products, arithmetic and copies ran while one was open for 46% -> 2% of each run, Pallas kernels for 0% -> 10%
where the time goes in v1:
time: 402 us
  waiting for transfers between devices  178 us (44%)
  blocking collectives  97.3 us (24%)
  Pallas kernels  85.2 us (21%)
  starting transfers between devices  15.7 us (4%)
  between operations  13.4 us (3%)
  local copies, waits for them, and re-layouts  11.4 us (3%)
    all_to_all x1, blocking collectives, on_device(): lax.all_to_all(done, 'seq', split_axis=0, concat_axis=0, tiled=True)  97.3 us
    all_to_all x1, waiting for transfers between devices, on_device(): lax.all_to_all(outgoing.reshape(n_seq, exp_dev, capacity, channels), 'seq...  54.3 us
    all_to_all x1, waiting for transfers between devices, on_device(): lax.all_to_all(summed, 'seq', split_axis=0, concat_axis=0, tiled=True)  45.9 us
    all_to_all x1, waiting for transfers between devices, on_device(): lax.all_to_all(turned, 'seq', split_axis=0, concat_axis=0, tiled=True)  39.4 us
    all_gather x1, waiting for transfers between devices, on_device(): all_out = lax.all_gather(w_out, 'batch', axis=0, tiled=False)  37.5 us
    pallas_call x1, Pallas kernels, norm_and_send(): pl.pallas_call(functools.partial(norm_kernel, blocks), in_specs=[vmem] *...  26.3 us
    pallas_call x1, Pallas kernels, finish(): pl.pallas_call(finish_kernel, grid=(tokens // INNER,), in_specs=[pl.Block...  24.1 us
    pallas_call x1, Pallas kernels, spectral(): pl.pallas_call(functools.partial(spectral_kernel, chans, outer), grid=(ch...  14 us
  transfers between devices with their start and end apart: 5, of which 4 were waited for; matrix products, arithmetic and copies ran while one was open for 2% of the time, Pallas kernels for 10%

profile of v1, /device:TPU:0, one launch (start us, length us, event | category | flops | bytes accessed | tf_op | source)
XLA Modules:
  0.0 401.5 jit_solution(14378847416516280060)
XLA Ops:
  6.5 5.1 %turn.1 = bf16[4096,256]{1,0:T(8,128)(2,1)} custom-call(bf16[4096,256]{1,0:T(8,128)(2,1)} %bitcast.33), custom_call_target="tpu_custom_call" | custom-call | tf_op jit(solution)/shard_map/turn/pallas_call | solution.py:73
  11.6 7.3 %all-to-all-start = ((bf16[8,32,16,256]{3,2,1,0:T(8,128)(2,1)}), bf16[8,32,16,256]{3,2,1,0:T(8,128)(2,1)S(1)}, u32[]{:S(2)}, u32[]{:S(2)}) async-start(bf16[8,32,16,256]{3,2,1,0:T(8,128)(2,1)} %bitcast.28), calls=%async_computation | async-start | bytes 4194304 | tf_op jit(solution)/shard_map/all_to_all | solution.py:328
  18.8 0.0 all-gather.5.cloned.1.call-start
  18.9 0.7 all-gather.5.cloned.1.call-update
  19.6 8.1 %copy.21 = f32[8,8,256,128]{3,2,1,0:T(8,128)} copy(f32[8,8,256,128]{3,1,2,0:T(8,128)} %bitcast.27) | data formatting | bytes 16777216
  27.7 39.4 %all-to-all-done.x_ref = bf16[8,32,16,256]{3,2,1,0:T(8,128)(2,1)S(1)} async-done(((bf16[8,32,16,256]{3,2,1,0:T(8,128)(2,1)}), bf16[8,32,16,256]{3,2,1,0:T(8,128)(2,1)S(1)}, u32[]{:S(2)}, u32[]{:S(2)}) %all-to-all-start) | async-done | bytes 2097184 | tf_op jit(solution)/shard_map/all_to_all | solution.py:328
  67.1 0.0 copy-start
  67.1 1.3 copy-done
  68.4 14.0 %spectral.1 = bf16[8,32,16,256]{3,2,1,0:T(8,128)(2,1)} custom-call(bf16[8,32,16,256]{3,2,1,0:T(8,128)(2,1)} %copy-done, f32[2,32,256,128]{3,2,1,0:T(8,128)} %bitcast.25, bf16[256,128]{1,0:T(8,128)(2,1)} %constant.27.f1_ref, bf16[512,512]{1,0:T(8,128)(2,1)} %constant.28.m2_ref, bf16[512,512]{1,0:T(8,128)(2,1)} %constant.29.m3_ref, ...), custom_call_target="tpu_custom_call" | custom-call | tf_op jit(solution)/shard_map/spectral/pallas_call | solution.py:130
  82.4 0.0 copy-start.2
  82.4 3.8 all-to-all-start.1
  86.1 1.9 slots.1.slot_ref
  88.0 0.0 copy-done.2
  88.0 0.7 copy.23
  88.7 45.9 %all-to-all-done.1 = bf16[8,32,16,256]{3,2,1,0:T(8,128)(2,1)S(1)} async-done(((bf16[8,32,16,256]{3,2,1,0:T(8,128)(2,1)}), bf16[8,32,16,256]{3,2,1,0:T(8,128)(2,1)S(1)}, u32[]{:S(2)}, u32[]{:S(2)}) %all-to-all-start.1) | async-done | bytes 2097184 | tf_op jit(solution)/shard_map/all_to_all | solution.py:336
  134.6 0.0 copy-start.1
  134.6 1.3 copy-done.1
  135.9 26.3 %norm.1 = (bf16[8192,256]{1,0:T(8,128)(2,1)}, f32[8,4096]{1,0:T(8,128)}) custom-call(bf16[4096,256]{1,0:T(8,128)(2,1)} %bitcast.29, f32[1,256]{1,0:T(1,128)} %bitcast.38, bf16[192,256]{1,0:T(8,128)(2,1)} %bitcast.35, s32[1,4096]{1,0:T(1,128)} %bitcast.37, s32[3,4096]{1,0:T(4,128)} %bitcast.34, s32[1,4096]{1,0:T(1,128)} %slots.1.slot_ref, f32[3,16]{1,0:T(4,128)} %table_ref.1), custom_call_target="tpu_custom_call" | custom-call | tf_op jit(solution)/shard_map/norm/pallas_call | solution.py:225
  162.2 4.5 %all-to-all-start.2 = ((bf16[8,8,128,256]{3,2,1,0:T(8,128)(2,1)}), bf16[8,8,128,256]{3,2,1,0:T(8,128)(2,1)}, u32[]{:S(2)}, u32[]{:S(2)}) async-start(bf16[8,8,128,256]{3,2,1,0:T(8,128)(2,1)} %bitcast.30), calls=%async_computation.2 | async-start | bytes 8388608 | tf_op jit(solution)/shard_map/all_to_all | solution.py:347
  166.8 0.0 all-gather.7.cloned.1.call-start
  166.8 0.7 all-gather.7.cloned.1.call-update
  167.5 0.0 all-gather.5.cloned.1.call-done
  167.6 37.5 %all-gather.7.cloned.1.call-done = bf16[32,256,256]{2,1,0:T(8,128)(2,1)} async-done(((bf16[8,256,256]{2,1,0:T(8,128)(2,1)}), bf16[32,256,256]{2,1,0:T(8,128)(2,1)}) %all-gather.7.cloned.1.call-update) | async-done | bytes 4194320 | tf_op jit(solution)/shard_map/all_gather | solution.py:325
  205.0 54.3 %all-to-all-done.2.x_ref = bf16[8,8,128,256]{3,2,1,0:T(8,128)(2,1)} async-done(((bf16[8,8,128,256]{3,2,1,0:T(8,128)(2,1)}), bf16[8,8,128,256]{3,2,1,0:T(8,128)(2,1)}, u32[]{:S(2)}, u32[]{:S(2)}) %all-to-all-start.2) | async-done | bytes 4194336 | tf_op jit(solution)/shard_map/all_to_all | solution.py:347
  259.3 13.9 %experts.1 = bf16[8,8,128,256]{3,2,1,0:T(8,128)(2,1)} custom-call(bf16[8,8,128,256]{3,2,1,0:T(8,128)(2,1)} %all-to-all-done.2.x_ref, bf16[4,8,256,256]{3,2,1,0:T(8,128)(2,1)} %bitcast.31, bf16[4,8,256,256]{3,2,1,0:T(8,128)(2,1)} %bitcast.32), custom_call_target="tpu_custom_call" | custom-call | tf_op jit(solution)/shard_map/experts/pallas_call | solution.py:257
  273.2 97.3 %all_to_all.20 = bf16[8,8,128,256]{3,2,1,0:T(8,128)(2,1)} all-to-all(bf16[8,8,128,256]{3,2,1,0:T(8,128)(2,1)} %experts.1), channel_id=1, replica_groups=mesh['seq'=8,'batch'=4] {'seq'}, dimensions={0} | all-to-all | bytes 8388608 | tf_op jit(solution)/shard_map/all_to_all | solution.py:352
  370.6 24.1 %finish.1 = bf16[3,4096,256]{2,1,0:T(8,128)(2,1)} custom-call(bf16[8192,256]{1,0:T(8,128)(2,1)} %bitcast.26, f32[8,4096]{1,0:T(8,128)} %get-tuple-element.8.gate_ref, s32[1,4096]{1,0:T(1,128)} %slots.1.slot_ref), custom_call_target="tpu_custom_call" | custom-call | tf_op jit(solution)/shard_map/finish/pallas_call | solution.py:293
Async XLA Ops:
  11.6 55.5 %all-to-all-start = ((bf16[8,32,16,256]{3,2,1,0:T(8,128)(2,1)}), bf16[8,32,16,256]{3,2,1,0:T(8,128)(2,1)S(1)}, u32[]{:S(2)}, u32[]{:S(2)}) async-start(bf16[8,32,16,256]{3,2,1,0:T(8,128)(2,1)} %bitcast.28), calls=%async_computation | async-start | bytes 4194304 | tf_op jit(solution)/shard_map/all_to_all | solution.py:328
  18.8 148.7 %all-gather.5.cloned.1.call-start = ((), (), s32[]{:S(2)}) async-start(), calls=%async_computation.4 | async-start | bytes 5242880 | tf_op jit(solution)/shard_map/all_gather | solution.py:324
  67.1 1.3 copy-start
  82.4 5.6 %copy-start.2 = (s32[1,4096,1,3]{1,2,3,0:T(1,128)S(1)}, s32[1,4096,1,3]{1,2,3,0:T(1,128)}, u32[]{:S(2)}) copy-start(s32[1,4096,1,3]{1,2,3,0:T(1,128)} %param.25) | copy-start | bytes 147460
  82.4 52.2 %all-to-all-start.1 = ((bf16[8,32,16,256]{3,2,1,0:T(8,128)(2,1)}), bf16[8,32,16,256]{3,2,1,0:T(8,128)(2,1)S(1)}, u32[]{:S(2)}, u32[]{:S(2)}) async-start(bf16[8,32,16,256]{3,2,1,0:T(8,128)(2,1)} %spectral.1), calls=%async_computation.1 | async-start | bytes 4194304 | tf_op jit(solution)/shard_map/all_to_all | solution.py:336
  134.6 1.3 copy-start.1
  162.2 97.1 %all-to-all-start.2 = ((bf16[8,8,128,256]{3,2,1,0:T(8,128)(2,1)}), bf16[8,8,128,256]{3,2,1,0:T(8,128)(2,1)}, u32[]{:S(2)}, u32[]{:S(2)}) async-start(bf16[8,8,128,256]{3,2,1,0:T(8,128)(2,1)} %bitcast.30), calls=%async_computation.2 | async-start | bytes 8388608 | tf_op jit(solution)/shard_map/all_to_all | solution.py:347
  166.8 38.3 %all-gather.7.cloned.1.call-start = ((), (), s32[]{:S(2)}) async-start(), calls=%async_computation.5 | async-start | bytes 5242880 | tf_op jit(solution)/shard_map/all_gather | solution.py:325
Sparse Core Ops, SparseCore 0:
  21.2 35.9 all-gather.4
  169.2 35.8 all-gather.6

commit v2 on v1

v2 whole, which is shorter than its diff:
```python
import functools
import math

import jax
import jax.numpy as jnp
import numpy as np
from jax import lax
from jax.experimental import pallas as pl
from jax.experimental.pallas import tpu as pltpu
from jax.sharding import PartitionSpec as P

EXPERTS = 64
TASKS = 3
INNER = 256
LANES = 128
ROWS = 16
VMEM_BYTES = 56 * 2**20
F32 = jnp.float32
BF16 = jnp.bfloat16


def params():
    return pltpu.CompilerParams(vmem_limit_bytes=VMEM_BYTES)


def dot_nt(a, b):
    return lax.dot_general(a, b, (((1,), (1,)), ((), ())), preferred_element_type=F32)


def dot_nn(a, b):
    return jnp.dot(a, b, preferred_element_type=F32)


def tables(length):
    outer = length // INNER

    def angles(rows, cols, points):
        product = np.outer(np.arange(rows), np.arange(cols)) % points
        return product * (2.0 * np.pi / points)

    first = angles(outer, outer, outer)
    inner = angles(INNER, INNER, INNER)
    turn = angles(outer, INNER, length)
    c1, s1, c2, s2 = np.cos(first), np.sin(first), np.cos(inner), np.sin(inner)
    f1 = np.concatenate([c1, -s1], 0)
    m2 = np.block([[c2, s2], [-s2, c2]])
    m3 = np.block([[c2, -s2], [s2, c2]])
    f4 = np.concatenate([c1, -s1], 1) / length
    def bf(a):
        near = a.astype(jnp.bfloat16)
        rest = (a - near.astype(np.float64)).astype(jnp.bfloat16)
        return jnp.asarray(np.stack([near, rest]))

    fl = lambda a: jnp.asarray(a.astype(np.float32))
    return (
        bf(f1), bf(m2), bf(m3), bf(f4),
        fl(np.cos(turn)), fl(np.sin(turn)), fl(np.cos(turn).T), fl(np.sin(turn).T),
    )


def turn_kernel(blocks, parts, x_ref, *refs):
    outs, low, high = refs[:parts], refs[parts], refs[parts + 1]

    def step(j, _):
        rows = x_ref[pl.ds(pl.multiple_of(j * INNER, INNER), INNER), :]
        turned = rows.astype(F32).T
        low[pl.ds(j, LANES, stride=blocks), :] = turned[:, :LANES]
        high[pl.ds(j, LANES, stride=blocks), :] = turned[:, LANES:]
        return 0

    lax.fori_loop(0, blocks, step, 0, unroll=2)
    dests, rows, _ = outs[0].shape
    for part in range(parts):
        for side, half in enumerate((low, high)):
            value = half[...].reshape(dests, parts, rows, LANES)[:, part]
            outs[part][:, :, side * LANES:(side + 1) * LANES] = value.astype(BF16)


def turn(events, chan_dev, parts):
    tokens, channels = events.shape
    blocks = tokens // INNER
    rows = chan_dev // parts * blocks
    dests = LANES // chan_dev
    return pl.pallas_call(
        functools.partial(turn_kernel, blocks, parts),
        grid=(channels // LANES,),
        in_specs=[pl.BlockSpec((tokens, LANES), lambda i: (0, i))],
        out_specs=[pl.BlockSpec((dests, rows, INNER), lambda i: (i, 0, 0))] * parts,
        out_shape=[jax.ShapeDtypeStruct((channels // chan_dev, rows, INNER), BF16)] * parts,
        scratch_shapes=[pltpu.VMEM((LANES * blocks, LANES), F32)] * 2,
        compiler_params=params(),
        name="turn",
    )(events)


def spectral_kernel(
    chans, outer, x_ref, h_ref, f1_ref, m2_ref, m3_ref, f4_ref, tc, ts, tct, tst, out_ref,
    y_ref, g_ref,
):
    x_all = x_ref[...]
    for c in range(chans):
        x = x_all[:, c].reshape(outer, INNER)
        a = dot_nn(f1_ref[0], x) + dot_nn(f1_ref[1], x)
        re, im = a[:outer], a[outer:]
        rows = slice(c * outer, (c + 1) * outer)
        y_ref[rows, :INNER] = (re * tc[...] + im * ts[...]).astype(BF16)
        y_ref[rows, INNER:] = (im * tc[...] - re * ts[...]).astype(BF16)
    y_all = y_ref[...]
    z = dot_nt(m2_ref[0], y_all) + dot_nt(m2_ref[1], y_all)
    for c in range(chans):
        cols = slice(c * outer, (c + 1) * outer)
        zr, zi = z[:INNER, cols], z[INNER:, cols]
        hr, hi = h_ref[0, c], h_ref[1, c]
        g_ref[:INNER, cols] = (zr * hr - zi * hi).astype(BF16)
        g_ref[INNER:, cols] = (zr * hi + zi * hr).astype(BF16)
    g_all = g_ref[...]
    u = dot_nn(m3_ref[0], g_all) + dot_nn(m3_ref[1], g_all)
    for c in range(chans):
        cols = slice(c * outer, (c + 1) * outer)
        ur, ui = u[:INNER, cols], u[INNER:, cols]
        v = jnp.concatenate(
            [
                (ur * tct[...] - ui * tst[...]).astype(BF16),
                (ui * tct[...] + ur * tst[...]).astype(BF16),
            ],
            1,
        )
        y = dot_nt(f4_ref[0], v) + dot_nt(f4_ref[1], v)
        x = x_all[:, c].reshape(outer, INNER)
        total = (x.astype(F32) + y).astype(BF16)
        out_ref[:, c] = total.reshape(out_ref.shape[0], out_ref.shape[2], INNER)


def spectral(x, filt, part):
    parts, chan_dev, blocks, _ = x.shape
    length = parts * blocks * INNER
    outer = length // INNER
    chans = math.gcd(chan_dev, 4)
    consts = tables(length)
    first = part * (chan_dev // chans)
    whole = lambda a: pl.BlockSpec(a.shape, lambda i: (0,) * a.ndim)
    x_spec = pl.BlockSpec((parts, chans, blocks, INNER), lambda i: (0, i, 0, 0))
    return pl.pallas_call(
        functools.partial(spectral_kernel, chans, outer),
        grid=(chan_dev // chans,),
        in_specs=[x_spec, pl.BlockSpec((2, chans, INNER, outer), lambda i: (0, first + i, 0, 0))]
        + [whole(a) for a in consts],
        out_specs=x_spec,
        out_shape=jax.ShapeDtypeStruct(x.shape, BF16),
        scratch_shapes=[
            pltpu.VMEM((chans * outer, 2 * INNER), BF16),
            pltpu.VMEM((2 * INNER, chans * outer), BF16),
        ],
        compiler_params=params(),
        cost_estimate=pl.CostEstimate(
            flops=chan_dev * 2 * 2 * (2 * outer * outer * INNER * 2 + 8 * INNER * INNER * outer),
            bytes_accessed=chan_dev * length * 12,
            transcendentals=0,
        ),
        name="spectral",
    )(x, filt, *consts)


def slot_kernel(exp_dev, reach, routes_ref, slot_ref, size_ref):
    tokens = routes_ref.shape[1]
    row = lax.broadcasted_iota(jnp.int32, (INNER, INNER), 0)
    col = lax.broadcasted_iota(jnp.int32, (INNER, INNER), 1)
    before = (row < col).astype(F32).astype(BF16)
    expert = lax.broadcasted_iota(jnp.int32, (EXPERTS, INNER), 0)

    def hot_of(j):
        return (expert == routes_ref[:, j * INNER:(j + 1) * INNER]).astype(F32)

    count = jnp.zeros((EXPERTS, 1), F32)
    for j in range(tokens // INNER):
        count = count + jnp.sum(hot_of(j), 1, keepdims=True)
    size = jnp.floor((count + (ROWS - 1)) * (1.0 / ROWS)) * ROWS
    wide = jnp.broadcast_to(size, (EXPERTS, LANES))
    size_ref[...] = wide.astype(jnp.int32)
    mine = lax.broadcasted_iota(jnp.int32, (EXPERTS, EXPERTS), 0)
    other = lax.broadcasted_iota(jnp.int32, (EXPERTS, EXPERTS), 1)
    same = lax.div(mine, exp_dev) == lax.div(other, exp_dev)
    earlier = jnp.where(same & (other < mine), 1.0, 0.0).astype(BF16)
    offset = dot_nn(earlier, wide.astype(BF16))[:, :1]
    owner = lax.div(lax.broadcasted_iota(jnp.int32, (EXPERTS, 1), 0), exp_dev)
    base = offset + (owner * reach).astype(F32)
    for j in range(tokens // INNER):
        hot = hot_of(j)
        rank = dot_nn(hot.astype(BF16), before)
        value = jnp.sum(hot * (rank + base), 0, keepdims=True)
        slot_ref[:, j * INNER:(j + 1) * INNER] = value.astype(jnp.int32)
        base = base + jnp.sum(hot, 1, keepdims=True)


def slots_of(routes, exp_dev, reach):
    return pl.pallas_call(
        functools.partial(slot_kernel, exp_dev, reach),
        out_shape=[
            jax.ShapeDtypeStruct(routes.shape, jnp.int32),
            jax.ShapeDtypeStruct((EXPERTS, LANES), jnp.int32),
        ],
        compiler_params=params(),
        name="slots",
    )(routes)


def norm_kernel(
    blocks, parts, chunks, *refs
):
    x_refs, refs = refs[:parts], refs[parts:]
    gain_ref, gw_ref, routes_ref, gi_ref, slot_ref, table_ref, *refs = refs
    out_refs, refs = refs[:chunks], refs[chunks:]
    gate_ref, low, high, rows_ref, spread = refs
    channels = gain_ref.shape[1]
    sources, rows, _ = x_refs[0].shape
    for source in range(sources):
        for part in range(parts):
            x = x_refs[part][source].astype(F32)
            at = pl.ds((source * parts + part) * rows, rows)
            low[at, :] = x[:, :LANES]
            high[at, :] = x[:, LANES:]
    expert = lax.broadcasted_iota(jnp.int32, (EXPERTS, INNER), 0)

    def step(j, _):
        start = pl.multiple_of(j * INNER, INNER)
        t = jnp.concatenate(
            [
                low[pl.ds(j, channels, stride=blocks), :],
                high[pl.ds(j, channels, stride=blocks), :],
            ],
            1,
        )
        centre = jnp.sum(t, 0, keepdims=True) * (1.0 / channels)
        away = t - centre
        var = jnp.sum(away * away, 0, keepdims=True) * (1.0 / channels)
        scaled = away * lax.rsqrt(var + 1e-05)
        normed = (scaled.T * gain_ref[...]).astype(BF16)
        rows_ref[...] = normed.astype(F32)
        scores = dot_nt(gw_ref[...], normed)
        hot = expert == routes_ref[:, pl.ds(start, INNER)]
        for task in range(TASKS):
            part = scores[task * EXPERTS:(task + 1) * EXPERTS]
            chosen = jnp.sum(jnp.where(hot, part, 0.0), 0, keepdims=True)
            index = gi_ref[task:task + 1, pl.ds(start, INNER)]
            bias = jnp.zeros((1, INNER), F32)
            for entry in range(table_ref.shape[1]):
                bias = jnp.where(index == entry, table_ref[task, entry], bias)
            logit = chosen.astype(BF16).astype(F32) + bias
            gate_ref[task:task + 1, pl.ds(start, INNER)] = jax.nn.sigmoid(logit)

        def move(i, _):
            for u in range(16):
                n = i * 16 + u
                spread[pl.ds(slot_ref[0, start + n], 1), :] = rows_ref[pl.ds(n, 1), :]
            return 0

        lax.fori_loop(0, INNER // 16, move, 0)
        return 0

    lax.fori_loop(0, blocks, step, 0)
    size = spread.shape[0] // chunks
    for chunk in range(chunks):
        out_refs[chunk][...] = spread[chunk * size:(chunk + 1) * size, :].astype(BF16)


def norm_and_send(xs, gain, gate_cols, routes, index, slot, table, slot_total, chunks):
    channels = gain.shape[1]
    parts = len(xs)
    tokens = routes.shape[1]
    blocks = tokens // INNER
    vmem = pl.BlockSpec(memory_space=pltpu.VMEM)
    smem = pl.BlockSpec(memory_space=pltpu.SMEM)
    return pl.pallas_call(
        functools.partial(norm_kernel, blocks, parts, chunks),
        in_specs=[vmem] * (parts + 4) + [smem] * 2,
        out_specs=[vmem] * (chunks + 1),
        out_shape=[jax.ShapeDtypeStruct((slot_total // chunks, channels), BF16)] * chunks
        + [jax.ShapeDtypeStruct((8, tokens), F32)],
        scratch_shapes=[
            pltpu.VMEM((channels * blocks, LANES), F32),
            pltpu.VMEM((channels * blocks, LANES), F32),
            pltpu.VMEM((INNER, channels), F32),
            pltpu.VMEM((slot_total, channels), F32),
        ],
        compiler_params=params(),
        name="norm",
    )(*xs, gain, gate_cols, routes, index, slot, table)


def expert_kernel(chunk, x_ref, w_in_ref, w_out_ref, start_ref, size_ref, out_ref, held, made):
    e = pl.program_id(0)
    sources, height, channels = x_ref.shape

    def piece(source):
        start = start_ref[source, e] - chunk * height
        low = jnp.clip(start, 0, height)
        high = jnp.clip(start + size_ref[source, e], 0, height)
        return low, lax.div(high - low, ROWS)

    def at(first, i):
        return pl.ds(pl.multiple_of(first + i * ROWS, ROWS), ROWS)

    def fetch(source, filled):
        low, count = piece(source)

        def one(i, _):
            held[at(filled, i), :] = x_ref[source, at(low, i), :]
            return 0

        lax.fori_loop(0, count, one, 0)
        return filled + count * ROWS

    total = lax.fori_loop(0, sources, fetch, 0)
    w_in = w_in_ref[...].reshape(-1, channels)
    w_out = w_out_ref[...].reshape(-1, channels)

    def tile(t, _):
        rows = pl.ds(pl.multiple_of(t * INNER, INNER), INNER)
        hidden = jnp.maximum(dot_nt(held[rows, :], w_in), 0.0).astype(BF16)
        made[rows, :] = dot_nn(hidden, w_out).astype(BF16)
        return 0

    lax.fori_loop(0, lax.div(total + INNER - 1, INNER), tile, 0)

    def give(source, filled):
        low, count = piece(source)

        def one(i, _):
            out_ref[source, at(low, i), :] = made[at(filled, i), :]
            return 0

        lax.fori_loop(0, count, one, 0)
        return filled + count * ROWS

    lax.fori_loop(0, sources, give, 0)


def experts(x, w_in, w_out, start, size, chunk, chunks, capacity):
    sources, height, channels = x.shape
    shares, count, hid, _ = w_in.shape
    most = -(-sources * capacity // INNER) * INNER
    x_spec = pl.BlockSpec(x.shape, lambda e: (0, 0, 0))
    w_spec = pl.BlockSpec((shares, 1, hid, channels), lambda e: (0, e, 0, 0))
    smem = pl.BlockSpec(memory_space=pltpu.SMEM)
    return pl.pallas_call(
        functools.partial(expert_kernel, chunk),
        grid=(count,),
        in_specs=[x_spec, w_spec, w_spec, smem, smem],
        out_specs=x_spec,
        out_shape=jax.ShapeDtypeStruct(x.shape, BF16),
        scratch_shapes=[pltpu.VMEM((most, channels), BF16)] * 2,
        compiler_params=params(),
        cost_estimate=pl.CostEstimate(
            flops=4 * sources * height * channels * shares * hid,
            bytes_accessed=2 * (2 * x.size + w_in.size + w_out.size),
            transcendentals=0,
        ),
        name="experts",
    )(x, w_in, w_out, start, size)


def finish_kernel(chunks, *refs):
    res_refs, refs = refs[:chunks], refs[chunks:]
    gate_ref, slot_ref, out_ref, wide, rows_ref = refs
    j = pl.program_id(0)

    @pl.when(j == 0)
    def _():
        size = res_refs[0].shape[0]
        for chunk in range(chunks):
            wide[chunk * size:(chunk + 1) * size, :] = res_refs[chunk][...].astype(F32)

    start = j * INNER

    def move(i, _):
        for u in range(16):
            n = i * 16 + u
            rows_ref[pl.ds(n, 1), :] = wide[pl.ds(slot_ref[0, start + n], 1), :]
        return 0

    lax.fori_loop(0, INNER // 16, move, 0)
    gates = gate_ref[...].T
    rows = rows_ref[...]
    for task in range(TASKS):
        out_ref[task] = (gates[:, task:task + 1] * rows).astype(BF16)


def finish(results, gates, slot):
    chunks = len(results)
    size, channels = results[0].shape
    tokens = gates.shape[1]
    return pl.pallas_call(
        functools.partial(finish_kernel, chunks),
        grid=(tokens // INNER,),
        in_specs=[pl.BlockSpec((size, channels), lambda j: (0, 0))] * chunks
        + [
            pl.BlockSpec((8, INNER), lambda j: (0, j)),
            pl.BlockSpec(memory_space=pltpu.SMEM),
        ],
        out_specs=pl.BlockSpec((TASKS, INNER, channels), lambda j: (0, j, 0)),
        out_shape=jax.ShapeDtypeStruct((TASKS, tokens, channels), BF16),
        scratch_shapes=[
            pltpu.VMEM((chunks * size, channels), F32),
            pltpu.VMEM((INNER, channels), F32),
        ],
        compiler_params=params(),
        name="finish",
    )(*results, gates, slot)


def on_device(
    events, spectral_filter, ln_gain, w_in, w_out, gate_weight, gate_table, routes, gate_index
):
    n_seq = lax.axis_size("seq")
    _, len_dev, user_count, channels = events.shape
    chan_dev = channels // n_seq
    blocks = len_dev // INNER
    capacity = max(2, 2 * len_dev // EXPERTS)
    exp_dev = w_in.shape[0]
    reach = exp_dev * capacity
    parts = 2 if chan_dev % 16 == 0 and blocks % 16 == 0 else 1
    route_row = routes.reshape(1, len_dev)
    index_rows = gate_index.reshape(len_dev, TASKS).T
    gate_cols = gate_weight.transpose(0, 2, 1).reshape(TASKS * EXPERTS, channels)

    slot, size = slots_of(route_row, exp_dev, reach)
    sizes = lax.all_gather(size[:, 0], ("batch", "seq"), axis=0, tiled=False)
    heights = tier_heights(reach)
    tallest = jnp.max(jnp.sum(sizes.reshape(-1, n_seq, exp_dev), -1))
    tier = sum((tallest > height).astype(jnp.int32) for height in heights[:-1])
    own = lax.dynamic_slice(
        sizes,
        (lax.axis_index("batch") * n_seq, lax.axis_index("seq") * exp_dev),
        (n_seq, exp_dev),
    )
    ahead = jnp.arange(exp_dev)[:, None] > jnp.arange(exp_dev)[None, :]
    start = jnp.sum(jnp.where(ahead[None], own[:, None, :], 0), -1)
    all_in = lax.all_gather(w_in, "batch", axis=0, tiled=False)
    all_out = lax.all_gather(w_out, "batch", axis=0, tiled=False)

    length = len_dev * n_seq
    filt = spectral_filter.transpose(0, 2, 1).reshape(2, chan_dev, INNER, length // INNER)
    chan_part = chan_dev // parts
    returned = []
    for part, turned in enumerate(turn(events.reshape(len_dev, channels), chan_dev, parts)):
        history = lax.all_to_all(turned, "seq", split_axis=0, concat_axis=0, tiled=True)
        history = history.reshape(n_seq, chan_part, blocks, INNER)
        if blocks % 16:
            merged = history.transpose(1, 0, 2, 3).reshape(1, chan_part, n_seq * blocks, INNER)
            summed = spectral(merged, filt, part)
            summed = summed.reshape(chan_part, n_seq, blocks, INNER).transpose(1, 0, 2, 3)
        else:
            summed = spectral(history, filt, part)
        summed = summed.reshape(n_seq, chan_part * blocks, INNER)
        returned.append(
            lax.all_to_all(summed, "seq", split_axis=0, concat_axis=0, tiled=True)
        )

    def mixture(height, returned, slot, start, own, all_in, all_out):
        chunks = 2 if height % (2 * ROWS) == 0 else 1
        chunk_rows = height // chunks
        owner, local = slot // reach, slot % reach
        chunk_of = local // chunk_rows
        place = (chunk_of * n_seq + owner) * chunk_rows + local % chunk_rows
        *outgoing, gates = norm_and_send(
            returned,
            ln_gain.reshape(1, channels),
            gate_cols,
            route_row,
            index_rows,
            place,
            gate_table,
            n_seq * height,
            chunks,
        )
        results = []
        for chunk, rows in enumerate(outgoing):
            arrived = lax.all_to_all(
                rows.reshape(n_seq, chunk_rows, channels),
                "seq", split_axis=0, concat_axis=0, tiled=True,
            )
            done = experts(arrived, all_in, all_out, start, own, chunk, chunks, capacity)
            back = lax.all_to_all(done, "seq", split_axis=0, concat_axis=0, tiled=True)
            results.append(back.reshape(n_seq * chunk_rows, channels))
        return finish(results, gates, place)

    branches = [functools.partial(mixture, height) for height in heights]
    task_out = lax.switch(tier, branches, returned, slot, start, own, all_in, all_out)
    return task_out.reshape(TASKS, 1, len_dev, user_count, channels)


def tier_heights(reach):
    if reach % 1024:
        return [reach]
    return [reach // 32 * share for share in (22, 23, 24, 26, 28, 32)]


def solution(mesh):
    in_specs = (
        P("batch", "seq", None, None),
        P(None, None, "seq"),
        P(),
        P("seq", "batch", None),
        P("seq", "batch", None),
        P(),
        P(),
        P("batch", "seq", None, None),
        P("batch", "seq", None, None),
    )
    out_specs = P(None, "batch", "seq", None, None)
    return jax.shard_map(
        on_device, mesh=mesh, in_specs=in_specs, out_specs=out_specs, check_vma=False
    )
```

time: 402 us -> 379 us (0.943)
  waiting for transfers between devices: 178 us -> 82.1 us
  Pallas kernels: 85.2 us -> 112 us
  blocking collectives: 97.3 us -> 124 us
  starting transfers between devices: 15.7 us -> 25.4 us
    unnamed x0 -> x1, blocking collectives: none -> 44.5 us
    all_gather x1, waiting for transfers between devices: 37.5 us -> 0.02 us  [on_device(): all_out = lax.all_gather(w_out, 'batch', axis=0, tiled=False)]
    all_to_all x1 -> x2, waiting for transfers between devices: 45.9 us -> 14.3 us  [on_device(): lax.all_to_all(summed, 'seq', split_axis=0, concat_axis=0, tiled=True)]
    all_to_all x1 -> x2, waiting for transfers between devices: 54.3 us -> 35.7 us  [the longest x1 18.6 us: mixture(): lax.all_to_all(rows.reshape(n_seq, chunk_rows, channels), 'seq', split_ax...]
    all_to_all x1 -> x2, blocking collectives: 97.3 us -> 79.1 us  [the longest x1 39.6 us: mixture(): back = lax.all_to_all(done, 'seq', split_axis=0, concat_axis=0, tiled=True)]
    pallas_call x5 -> x6, Pallas kernels: 71.3 us -> 88.7 us  [the longest x2 34.2 us: experts(): pl.pallas_call(functools.partial(expert_kernel, chunk), grid=(count,), in...]
    pallas_call x1 -> x2, Pallas kernels: 14 us -> 23.1 us  [spectral(): pl.pallas_call(functools.partial(spectral_kernel, chans, outer), grid=(ch...]
    all_to_all x1 -> x2, waiting for transfers between devices: 39.4 us -> 30.6 us  [on_device(): lax.all_to_all(turned, 'seq', split_axis=0, concat_axis=0, tiled=True)]
  transfers between devices with their start and end apart: 5 -> 8, of which waited for: 4 -> 5; matrix products, arithmetic and copies ran while one was open for 2% -> 3% of each run, Pallas kernels for 10% -> 17%
where the time goes in v2:
time: 379 us; the launch traced here: 375 us
  blocking collectives  124 us (33%)
  Pallas kernels  112 us (30%)
  waiting for transfers between devices  82.1 us (22%)
  starting transfers between devices  25.4 us (7%)
  between operations  17.4 us (5%)
  local copies, waits for them, and re-layouts  12 us (3%)
    unnamed x1, blocking collectives  44.5 us
    all_to_all x1, blocking collectives, mixture(): back = lax.all_to_all(done, 'seq', split_axis=0, concat_axis=0, tiled=True)  39.6 us
    all_to_all x1, blocking collectives, mixture(): lax.all_to_all(rows.reshape(n_seq, chunk_rows, channels), 'seq', split_ax...  39.4 us
    pallas_call x2, Pallas kernels, experts(): pl.pallas_call(functools.partial(expert_kernel, chunk), grid=(count,), in...  34.2 us
    all_to_all x2, waiting for transfers between devices, on_device(): lax.all_to_all(turned, 'seq', split_axis=0, concat_axis=0, tiled=True)  30.6 us
    pallas_call x1, Pallas kernels, norm_and_send(): pl.pallas_call(functools.partial(norm_kernel, blocks, parts, chunks), in_...  25 us
    pallas_call x1, Pallas kernels, finish(): pl.pallas_call(functools.partial(finish_kernel, chunks), grid=(tokens //...  23.7 us
    pallas_call x2, Pallas kernels, spectral(): pl.pallas_call(functools.partial(spectral_kernel, chans, outer), grid=(ch...  23.1 us
  transfers between devices with their start and end apart: 8, of which 5 were waited for; matrix products, arithmetic and copies ran while one was open for 3% of the time, Pallas kernels for 17%

profile of v2, /device:TPU:0, one launch (start us, length us, event | category | flops | bytes accessed | tf_op | source)
XLA Modules:
  0.0 375.5 jit_solution(2993434430621442195)
XLA Ops:
  6.5 0.7 all-gather.6.cloned.1.call-update
  7.3 5.0 %turn.1 = (bf16[8,256,256]{2,1,0:T(8,128)(2,1)}, bf16[8,256,256]{2,1,0:T(8,128)(2,1)}) custom-call(bf16[4096,256]{1,0:T(8,128)(2,1)} %bitcast.137), custom_call_target="tpu_custom_call" | custom-call | tf_op jit(solution)/shard_map/turn/pallas_call | solution.py:84
  12.3 7.3 %all-to-all-start.26 = ((bf16[8,256,256]{2,1,0:T(8,128)(2,1)}), bf16[8,256,256]{2,1,0:T(8,128)(2,1)S(1)}, u32[]{:S(2)}, u32[]{:S(2)}) async-start(bf16[8,256,256]{2,1,0:T(8,128)(2,1)} %get-tuple-element.338), calls=%async_computation.26 | async-start | bytes 2097152 | tf_op jit(solution)/shard_map/all_to_all | solution.py:446
  19.6 0.7 all-gather.8.cloned.1.call-update
  20.3 25.0 %all-to-all-done.26 = bf16[8,256,256]{2,1,0:T(8,128)(2,1)S(1)} async-done(((bf16[8,256,256]{2,1,0:T(8,128)(2,1)}), bf16[8,256,256]{2,1,0:T(8,128)(2,1)S(1)}, u32[]{:S(2)}, u32[]{:S(2)}) %all-to-all-start.26) | async-done | bytes 1048608 | tf_op jit(solution)/shard_map/all_to_all | solution.py:446
  45.3 3.6 all-to-all-start.24
  48.9 8.8 %copy.58 = f32[8,8,256,128]{3,2,1,0:T(8,128)} copy(f32[8,8,256,128]{3,1,2,0:T(8,128)} %bitcast.98) | data formatting | bytes 16777216
  57.7 11.6 %spectral.3 = bf16[8,16,16,256]{3,2,1,0:T(8,128)(2,1)} custom-call(bf16[8,16,16,256]{3,2,1,0:T(8,128)(2,1)} %bitcast.151, f32[2,32,256,128]{3,2,1,0:T(8,128)} %bitcast.99, bf16[2,256,128]{2,1,0:T(8,128)(2,1)} %constant.294.clone.f1_ref, bf16[2,512,512]{2,1,0:T(8,128)(2,1)} %constant.295.clone.m2_ref, bf16[2,512,512]{2,1,0:T(8,128)(2,1)} %constant.296.clone.m3_ref, ...), custom_call_target="tpu_custom_call" | custom-call | flops 5368709120 | bytes 6291456 | tf_op jit(solution)/shard_map/spectral/pallas_call | solution.py:143
  69.2 5.6 %all-to-all-done.24 = bf16[8,256,256]{2,1,0:T(8,128)(2,1)S(1)} async-done(((bf16[8,256,256]{2,1,0:T(8,128)(2,1)}), bf16[8,256,256]{2,1,0:T(8,128)(2,1)S(1)}, u32[]{:S(2)}, u32[]{:S(2)}) %all-to-all-start.24) | async-done | bytes 1048608 | tf_op jit(solution)/shard_map/all_to_all | solution.py:446
  74.8 3.6 all-to-all-start.27
  78.5 11.6 %spectral.2 = bf16[8,16,16,256]{3,2,1,0:T(8,128)(2,1)} custom-call(bf16[8,16,16,256]{3,2,1,0:T(8,128)(2,1)} %bitcast.150, f32[2,32,256,128]{3,2,1,0:T(8,128)} %bitcast.100, bf16[2,256,128]{2,1,0:T(8,128)(2,1)} %constant.294.clone.f1_ref, bf16[2,512,512]{2,1,0:T(8,128)(2,1)} %constant.295.clone.m2_ref, bf16[2,512,512]{2,1,0:T(8,128)(2,1)} %constant.296.clone.m3_ref, ...), custom_call_target="tpu_custom_call" | custom-call | flops 5368709120 | bytes 6291456 | tf_op jit(solution)/shard_map/spectral/pallas_call | solution.py:143
  90.1 14.3 %all-to-all-done.27 = bf16[8,256,256]{2,1,0:T(8,128)(2,1)S(1)} async-done(((bf16[8,256,256]{2,1,0:T(8,128)(2,1)}), bf16[8,256,256]{2,1,0:T(8,128)(2,1)S(1)}, u32[]{:S(2)}, u32[]{:S(2)}) %all-to-all-start.27) | async-done | bytes 1048608 | tf_op jit(solution)/shard_map/all_to_all | solution.py:456
  104.4 3.6 all-to-all-start.25
  108.1 0.9 slots.1
  110.2 0.9 slice_reduce_fusion
  111.4 44.5 %all-reduce = s32[2048]{0:T(1024)S(1)} all-reduce(s32[2048]{0:T(1024)S(1)} %dynamic-update-slice), channel_id=2, replica_groups=mesh['seq'=8,'batch'=4] {'batch','seq'}, use_global_device_ids=true, to_apply=%add | all-reduce | flops 2048 | bytes 16384
  156.1 0.6 reduce_sum.40
  156.7 0.6 reduce_max.9
  160.7 207.9 %conditional.1 = (bf16[3,1,4096,1,256]{4,2,3,1,0:T(8,128)(2,1)}) conditional(s32[]{:T(128)} %clamp.3, (f32[256]{0:T(256)S(1)}, bf16[3,64,256]{2,1,0:T(8,128)(2,1)S(1)}, s32[1,4096]{1,0:T(1,128)S(1)}, bf16[8,256,256]{2,1,0:T(8,128)(2,1)S(1)}, bf16[8,256,256]{2,1,0:T(8,128)(2,1)S(1)}, ...), branch_computations={%region_2.0_spmd, %region_4.6_spmd, %region_6.8_spmd, %region_8.10... | conditional | flops 8590107648 | bytes 62950244 | solution.py:488
  160.9 0.9 fusion.1.refs_6_.refs_3_
  161.8 25.0 %norm.7 = (bf16[2944,256]{1,0:T(8,128)(2,1)}, bf16[2944,256]{1,0:T(8,128)(2,1)}, f32[8,4096]{1,0:T(8,128)}) custom-call(bf16[8,256,256]{2,1,0:T(8,128)(2,1)S(1)} %get-tuple-element.251.refs_0_, bf16[8,256,256]{2,1,0:T(8,128)(2,1)S(1)} %get-tuple-element.252.refs_1_, f32[1,256]{1,0:T(1,128)S(1)} %bitcast.161, bf16[192,256]{1,0:T(8,128)(2,1)S(1)} %bitcast.126, ...), custom_call_target="tpu_custom_call" | custom-call | tf_op jit(solution)/shard_map/cond/branch_1_fun/norm/pallas_call | solution.py:273
  186.8 39.4 %all_to_all.118.x_ref = bf16[8,368,256]{2,1,0:T(8,128)(2,1)} all-to-all(bf16[8,368,256]{2,1,0:T(8,128)(2,1)} %bitcast.147), channel_id=1, replica_groups=mesh['seq'=8,'batch'=4] {'seq'}, dimensions={0} | all-to-all | bytes 3014656 | tf_op jit(solution)/shard_map/cond/branch_1_fun/all_to_all | solution.py:478
  226.2 3.6 all-to-all-start.4
  229.9 0.8 select_reduce_fusion.1.start_ref
  230.7 15.5 %experts.15 = bf16[8,368,256]{2,1,0:T(8,128)(2,1)} custom-call(bf16[8,368,256]{2,1,0:T(8,128)(2,1)} %all_to_all.118.x_ref, bf16[4,8,256,256]{3,2,1,0:T(8,128)(2,1)} %get-tuple-element.260.w_in_ref, bf16[4,8,256,256]{3,2,1,0:T(8,128)(2,1)} %get-tuple-element.261.w_out_ref, s32[8,8]{1,0:T(8,128)} %select_reduce_fusion.1.start_ref, s32[8,8]{1,0:T(8,128)} %copy-done.20), custom_call_target="tpu_custom_call" | custom-call | flops 3087007744 | bytes 11403264 | tf_op jit(solution)/shard_map/cond/branch_1_fun/experts/pallas_call | solution.py:345
  246.2 18.6 %all-to-all-done.4.x_ref = bf16[8,368,256]{2,1,0:T(8,128)(2,1)S(1)} async-done(((bf16[8,368,256]{2,1,0:T(8,128)(2,1)}), bf16[8,368,256]{2,1,0:T(8,128)(2,1)S(1)}, u32[]{:S(2)}, u32[]{:S(2)}) %all-to-all-start.4) | async-done | bytes 1507360 | tf_op jit(solution)/shard_map/cond/branch_1_fun/all_to_all | solution.py:478
  264.8 1.1 copy-done.12
  265.9 3.6 all-to-all-start.7
  269.6 18.7 %experts.14 = bf16[8,368,256]{2,1,0:T(8,128)(2,1)} custom-call(bf16[8,368,256]{2,1,0:T(8,128)(2,1)} %copy-done.12, bf16[4,8,256,256]{3,2,1,0:T(8,128)(2,1)} %get-tuple-element.260.w_in_ref, bf16[4,8,256,256]{3,2,1,0:T(8,128)(2,1)} %get-tuple-element.261.w_out_ref, s32[8,8]{1,0:T(8,128)} %select_reduce_fusion.1.start_ref, s32[8,8]{1,0:T(8,128)} %copy-done.20), custom_call_target="tpu_custom_call" | custom-call | flops 3087007744 | bytes 11403264 | tf_op jit(solution)/shard_map/cond/branch_1_fun/experts/pallas_call | solution.py:345
  288.2 17.1 %all-to-all-done.7 = bf16[8,368,256]{2,1,0:T(8,128)(2,1)S(1)} async-done(((bf16[8,368,256]{2,1,0:T(8,128)(2,1)}), bf16[8,368,256]{2,1,0:T(8,128)(2,1)S(1)}, u32[]{:S(2)}, u32[]{:S(2)}) %all-to-all-start.7) | async-done | bytes 1507360 | tf_op jit(solution)/shard_map/cond/branch_1_fun/all_to_all | solution.py:483
  305.3 39.6 %all_to_all.119 = bf16[8,368,256]{2,1,0:T(8,128)(2,1)} all-to-all(bf16[8,368,256]{2,1,0:T(8,128)(2,1)} %experts.14), channel_id=1, replica_groups=mesh['seq'=8,'batch'=4] {'seq'}, dimensions={0} | all-to-all | bytes 3014656 | tf_op jit(solution)/shard_map/cond/branch_1_fun/all_to_all | solution.py:483
  345.0 23.7 %finish.7 = bf16[3,4096,256]{2,1,0:T(8,128)(2,1)} custom-call(bf16[2944,256]{1,0:T(8,128)(2,1)} %bitcast.116, bf16[2944,256]{1,0:T(8,128)(2,1)} %bitcast.115, f32[8,4096]{1,0:T(8,128)} %get-tuple-element.266.refs_2_, s32[1,4096]{1,0:T(1,128)} %fusion.1.refs_6_.refs_3_), custom_call_target="tpu_custom_call" | custom-call | tf_op jit(solution)/shard_map/cond/branch_1_fun/finish/pallas_call | solution.py:392
  (36 shorter events, 1.3 us)
Async XLA Ops:
  6.5 154.1 %all-gather.6.cloned.1.call-start = ((), (), s32[]{:S(2)}) async-start(), calls=%async_computation.28 | async-start | bytes 5242880 | tf_op jit(solution)/shard_map/all_gather | solution.py:438
  12.3 33.0 %all-to-all-start.26 = ((bf16[8,256,256]{2,1,0:T(8,128)(2,1)}), bf16[8,256,256]{2,1,0:T(8,128)(2,1)S(1)}, u32[]{:S(2)}, u32[]{:S(2)}) async-start(bf16[8,256,256]{2,1,0:T(8,128)(2,1)} %get-tuple-element.338), calls=%async_computation.26 | async-start | bytes 2097152 | tf_op jit(solution)/shard_map/all_to_all | solution.py:446
  19.5 141.1 %all-gather.8.cloned.1.call-start = ((), (), s32[]{:S(2)}) async-start(), calls=%async_computation.29 | async-start | bytes 5242880 | tf_op jit(solution)/shard_map/all_gather | solution.py:439
  45.3 12.4 %copy-start.14 = (bf16[8,256,256]{2,1,0:T(8,128)(2,1)}, bf16[8,256,256]{2,1,0:T(8,128)(2,1)S(1)}, u32[]{:S(2)}) copy-start(bf16[8,256,256]{2,1,0:T(8,128)(2,1)S(1)} %all-to-all-done.26) | copy-start | bytes 3145732
  45.3 29.5 %all-to-all-start.24 = ((bf16[8,256,256]{2,1,0:T(8,128)(2,1)}), bf16[8,256,256]{2,1,0:T(8,128)(2,1)S(1)}, u32[]{:S(2)}, u32[]{:S(2)}) async-start(bf16[8,256,256]{2,1,0:T(8,128)(2,1)} %get-tuple-element.337), calls=%async_computation.24 | async-start | bytes 2097152 | tf_op jit(solution)/shard_map/all_to_all | solution.py:446
  74.8 3.6 copy-start.13
  74.8 29.6 %all-to-all-start.27 = ((bf16[8,256,256]{2,1,0:T(8,128)(2,1)}), bf16[8,256,256]{2,1,0:T(8,128)(2,1)S(1)}, u32[]{:S(2)}, u32[]{:S(2)}) async-start(bf16[8,256,256]{2,1,0:T(8,128)(2,1)} %bitcast.152), calls=%async_computation.27 | async-start | bytes 2097152 | tf_op jit(solution)/shard_map/all_to_all | solution.py:456
  90.1 18.0 %copy-start.15 = (s32[1,4096,1,1]{1,3,2,0:T(1,128)S(1)}, s32[1,4096,1,1]{1,3,2,0:T(1,128)}, u32[]{:S(2)}) copy-start(s32[1,4096,1,1]{1,3,2,0:T(1,128)} %param.38) | copy-start | bytes 49156
  90.1 18.9 %copy-start.25 = (u32[32]{0:T(128)S(1)}, u32[32]{0:T(128)}, u32[]{:S(2)}) copy-start(u32[32]{0:T(128)} %constant.307) | copy-start | bytes 388
  90.1 66.0 %copy-start.18 = (s32[1,4096,1,3]{1,2,3,0:T(1,128)S(1)}, s32[1,4096,1,3]{1,2,3,0:T(1,128)}, u32[]{:S(2)}) copy-start(s32[1,4096,1,3]{1,2,3,0:T(1,128)} %param.39) | copy-start | bytes 147460
  90.1 70.6 %copy-start.7 = (bf16[3,256,64]{1,2,0:T(8,128)(2,1)S(1)}, bf16[3,256,64]{1,2,0:T(8,128)(2,1)}, u32[]{:S(2)}) copy-start(bf16[3,256,64]{1,2,0:T(8,128)(2,1)} %param.36) | copy-start | bytes 294916
  90.1 70.6 %copy-start.16 = (f32[3,16]{1,0:T(4,128)S(1)}, f32[3,16]{1,0:T(4,128)}, u32[]{:S(2)}) copy-start(f32[3,16]{1,0:T(4,128)} %param.37) | copy-start | bytes 580
  90.1 70.6 %copy-start.19 = (f32[256]{0:T(256)S(1)}, f32[256]{0:T(256)}, u32[]{:S(2)}) copy-start(f32[256]{0:T(256)} %param.33) | copy-start | bytes 3076
  104.4 56.2 %all-to-all-start.25 = ((bf16[8,256,256]{2,1,0:T(8,128)(2,1)}), bf16[8,256,256]{2,1,0:T(8,128)(2,1)S(1)}, u32[]{:S(2)}, u32[]{:S(2)}) async-start(bf16[8,256,256]{2,1,0:T(8,128)(2,1)} %bitcast.149), calls=%async_computation.25 | async-start | bytes 2097152 | tf_op jit(solution)/shard_map/all_to_all | solution.py:456
  226.2 38.6 %all-to-all-start.4 = ((bf16[8,368,256]{2,1,0:T(8,128)(2,1)}), bf16[8,368,256]{2,1,0:T(8,128)(2,1)S(1)}, u32[]{:S(2)}, u32[]{:S(2)}) async-start(bf16[8,368,256]{2,1,0:T(8,128)(2,1)} %bitcast.146), calls=%async_computation.4 | async-start | bytes 3014656 | tf_op jit(solution)/shard_map/cond/branch_1_fun/all_to_all | solution.py:478
  229.9 0.8 copy-start.20
  264.8 1.1 copy-start.12
  265.9 39.4 %all-to-all-start.7 = ((bf16[8,368,256]{2,1,0:T(8,128)(2,1)}), bf16[8,368,256]{2,1,0:T(8,128)(2,1)S(1)}, u32[]{:S(2)}, u32[]{:S(2)}) async-start(bf16[8,368,256]{2,1,0:T(8,128)(2,1)} %experts.15), calls=%async_computation.7 | async-start | bytes 3014656 | tf_op jit(solution)/shard_map/cond/branch_1_fun/all_to_all | solution.py:483
  305.3 39.6 %copy-start.4 = (bf16[8,368,256]{2,1,0:T(8,128)(2,1)}, bf16[8,368,256]{2,1,0:T(8,128)(2,1)S(1)}, u32[]{:S(2)}) copy-start(bf16[8,368,256]{2,1,0:T(8,128)(2,1)S(1)} %all-to-all-done.7) | copy-start | bytes 4521988 | tf_op jit(solution)/shard_map/cond
Sparse Core Ops, SparseCore 0:
  8.9 37.1 all-gather.5
  47.7 34.4 all-gather.7
